TPU v7x, 768 devices: a whole 4x8x12 slice. The times are simulated.
768 devices in a mesh: blk: 384 (over x, y, z), grp: 2 (over core).
Axes of the slice: x: 4, y: 8, z: 12, core: 2. Of those that a mesh axis runs over, the one named last changes fastest.
Arguments:
- item_factors: bfloat16 [12288, 256], P(('blk', 'grp')), may hold values from -0.0546875 to 0.0546875
- user_start: float32 [98304, 256], P('blk'), may hold values from -6 to 6
- tile_items: int32 [384, 48], P('blk'), may hold values from 0 to 47, as said below
- tile_count: int32 [384], P('blk'), may hold values from 1 to 48, as said below
- tile_seed: int32 [384, 48], P('blk'), may hold values from 0 to 65520
Outputs:
- solution: float32 [98304, 256], P('blk', 'grp')
- residual: float32 [98304, 256], P('blk', 'grp')
Inputs may be any that keep to these rules, and one draw needn't show every extreme that they name: `tile_items`: each row is a permutation of the 48 item blocks. `tile_count`: skewed toward few heavy user blocks; some user block has all 48 slots live.
All inputs are finite; a program needn't handle non-finite values.
Results may differ from a plain program's by a relative error of at most 0.0095.
Values may be sent and summed in bfloat16 or wider, within the bound.
A program may use at most 64 MiB of HBM per device.

v0:
```python
import jax
import jax.numpy as jnp
from jax import lax
from jax.sharding import PartitionSpec as P

STEPS = 2


ridge_weight = 0.5


def confidence_tiles(seeds, row_count, tile_width, row_offset):
    row_ids = lax.broadcasted_iota(jnp.int32, (row_count, tile_width), 0) + row_offset
    col_ids = lax.broadcasted_iota(jnp.int32, (row_count, tile_width), 1)
    seed_grid = seeds[..., None, None]
    hashed = seed_grid % 65521 * 509 + row_ids * 7883 + col_ids * 6151
    hashed = hashed % 65521 * 32749 % 65521
    hashed = (hashed * 32749 + row_ids * 31 + col_ids * 17) % 65521
    observed = (hashed % 2).astype(jnp.float32)
    return observed * (0.5 + 0.0035 * (hashed // 2 % 1000).astype(jnp.float32))


def local_sweep(vector, gathered, item_sel, conf_all, live_turns, with_rhs, tile_width):
    nblocks = item_sel.shape[0]
    row_count = vector.shape[0] // nblocks
    stacked = vector.astype(jnp.bfloat16).reshape(nblocks, row_count, vector.shape[1])

    def one_block(packed):
        user_rows, item_row, conf_row, live_count = packed

        def add_slot(turn_index, running):
            turn_index = turn_index.astype(jnp.int32)
            item_block = lax.dynamic_slice_in_dim(
                gathered, item_row[turn_index] * tile_width, tile_width, 0
            )
            confidence = conf_row[turn_index]
            scores = lax.dot_general(
                user_rows, item_block, (((1,), (1,)), ((), ())), preferred_element_type=jnp.float32
            )
            weighted = (confidence * scores).astype(jnp.bfloat16)
            result = running - jnp.dot(weighted, item_block, preferred_element_type=jnp.float32)
            if with_rhs:
                target = jnp.where(confidence > 0.0, confidence + 1.0, 0.0).astype(jnp.bfloat16)
                result = result + jnp.dot(target, item_block, preferred_element_type=jnp.float32)
            return result

        return lax.fori_loop(0, live_count, add_slot, jnp.zeros(user_rows.shape, jnp.float32))

    return lax.map(one_block, (stacked, item_sel, conf_all, live_turns)).reshape(vector.shape)


def on_device(item_factors, user_start, tile_items, tile_count, tile_seed):
    core_index = lax.axis_index("grp")
    core_count = lax.axis_size("grp")
    full_rank = item_factors.shape[1]
    half_rank = full_rank // core_count
    nblocks = tile_items.shape[0]
    tile_width = user_start.shape[0] // nblocks
    gathered = lax.all_gather(item_factors, ("blk", "grp"), axis=0, tiled=True)
    partial_gram = lax.dot_general(
        item_factors, item_factors, (((0,), (0,)), ((), ())), preferred_element_type=jnp.float32
    )
    gram_matrix = lax.psum(partial_gram, ("blk", "grp"))
    shifted = gram_matrix + ridge_weight * jnp.eye(full_rank, dtype=jnp.float32)

    def operate_whole(vector):
        return jnp.dot(vector, shifted, precision=lax.Precision.HIGHEST)

    half_rows = tile_width // core_count
    row_offset = core_index * half_rows
    blocked = user_start.reshape(nblocks, tile_width, full_rank)
    mine = lax.dynamic_slice_in_dim(blocked, row_offset, half_rows, 1).reshape(
        nblocks * half_rows, full_rank
    )
    conf_all = confidence_tiles(tile_seed, half_rows, tile_width, row_offset)

    def own_sweep(vector, with_rhs):
        return local_sweep(vector, gathered, tile_items, conf_all, tile_count, with_rhs, tile_width)

    residual = own_sweep(mine, True) - operate_whole(mine)
    solution = mine
    direction = residual
    norm_now = jnp.sum(residual * residual, axis=1, keepdims=True)
    for number in range(STEPS):
        applied = operate_whole(direction) - own_sweep(direction, False)
        curvature = jnp.sum(direction * applied, axis=1, keepdims=True)
        step_size = norm_now / curvature
        solution = solution + step_size * direction
        residual = residual - step_size * applied
        norm_next = jnp.sum(residual * residual, axis=1, keepdims=True)
        direction = residual + norm_next / norm_now * direction
        norm_now = norm_next
    solution, residual = (
        lax.all_to_all(
            solution.reshape(nblocks, half_rows, full_rank),
            "grp",
            split_axis=2,
            concat_axis=1,
            tiled=True,
        ),
        lax.all_to_all(
            residual.reshape(nblocks, half_rows, full_rank),
            "grp",
            split_axis=2,
            concat_axis=1,
            tiled=True,
        ),
    )
    solution = solution.reshape(nblocks * tile_width, half_rank)
    residual = residual.reshape(nblocks * tile_width, half_rank)
    return (solution, residual)


def solution(mesh):
    return jax.shard_map(
        on_device,
        mesh=mesh,
        in_specs=(
            P(("blk", "grp"), None),
            P("blk", None),
            P("blk", None),
            P("blk"),
            P("blk", None),
        ),
        out_specs=(P("blk", "grp"), P("blk", "grp")),
        check_vma=False,
    )
```

profile of v0, /device:TPU:669, one launch (start us, length us, event | category | flops | bytes accessed | tf_op | source)
XLA Modules:
  0.0 982.1 jit_solution(13664387039310251253)
XLA Ops:
  8.0 1.7 fusion.69
  11.3 21.2 %fusion.40 = f32[48,128,256]{2,1,0:T(8,128)} fusion(s32[256]{0:T(256)S(1)} %get-tuple-element.237, s32[128]{0:T(128)S(1)} %get-tuple-element.235, s32[256]{0:T(256)S(1)} %get-tuple-element.238, s32[128]{0:T(128)S(1)} %get-tuple-element.236, s32[48]{0:T(128)S(1)} %fusion.57), kind=kLoop, calls=%fused_computation.51 | loop fusion | flops 84934656 | bytes 6294720 | tf_op jit(solution)/shard_map/mul | solution.py:20
  32.5 149.2 %all-gather.2.cloned.1.call-done = bf16[12288,256]{1,0:T(8,128)(2,1)} async-done(((bf16[16,256]{1,0:T(8,128)(2,1)}), bf16[12288,256]{1,0:T(8,128)(2,1)}) %all-gather.2.cloned.1.call-update) | async-done | bytes 6291472 | tf_op jit(solution)/shard_map/all_gather | solution.py:59
  181.7 215.1 %while.51 = (s32[]{:T(128)}, f32[128,256]{1,0:T(8,128)S(1)}, s32[]{:T(128)}, f32[48,128,256]{2,1,0:T(8,128)}, s32[48]{0:T(128)S(1)}, /*index=5*/bf16[12288,256]{...) while((s32[]{:T(128)}, f32[128,256]{1,0:T(8,128)S(1)}, ...), condition=%wide.region_1.2_spmd, body=%wide.region_0.0_spmd.sunk | while | flops 50593800 | bytes 1246945 | solution.py:47
  237.3 1.4 convolution_subtract_fusion.9
  246.2 1.4 convolution_subtract_fusion.9
  250.7 1.4 convolution_subtract_fusion.9
  331.1 1.4 convolution_subtract_fusion.9
  335.6 1.4 convolution_subtract_fusion.9
  353.5 1.4 convolution_subtract_fusion.9
  389.2 1.4 convolution_subtract_fusion.9
  396.9 248.5 %all-reduce.2.cloned.1.call-done = f32[256,256]{1,0:T(8,128)} async-done(((f32[256,256]{1,0:T(8,128)}), f32[256,256]{1,0:T(8,128)}) %all-reduce.2.cloned.1.call-update) | async-done | bytes 262160 | tf_op jit(solution)/shard_map/psum | solution.py:63
  646.7 158.6 %while.52 = (s32[]{:T(128)}, f32[128,256]{1,0:T(8,128)S(1)}, s32[]{:T(128)}, f32[48,128,256]{2,1,0:T(8,128)}, s32[48]{0:T(128)S(1)}, /*index=5*/bf16[12288,256]{...) while((s32[]{:T(128)}, f32[128,256]{1,0:T(8,128)S(1)}, ...), condition=%wide.region_5.6_spmd, body=%wide.region_4.5_spmd.sunk | while | flops 33652744 | bytes 722649 | solution.py:47
  648.6 1.4 convolution_subtract_fusion.10
  668.3 1.4 convolution_subtract_fusion.10
  698.0 1.4 convolution_subtract_fusion.10
  701.3 1.4 convolution_subtract_fusion.10
  714.4 1.4 convolution_subtract_fusion.10
  717.7 1.4 convolution_subtract_fusion.10
  721.0 1.4 convolution_subtract_fusion.10
  747.3 1.4 convolution_subtract_fusion.10
  750.6 1.4 convolution_subtract_fusion.10
  757.2 1.4 convolution_subtract_fusion.10
  773.7 1.4 convolution_subtract_fusion.10
  777.0 1.4 convolution_subtract_fusion.10
  790.1 1.4 convolution_subtract_fusion.10
  793.4 1.4 convolution_subtract_fusion.10
  796.7 1.4 convolution_subtract_fusion.10
  807.0 158.6 %while.53 = (s32[]{:T(128)}, f32[128,256]{1,0:T(8,128)S(1)}, s32[]{:T(128)}, f32[48,128,256]{2,1,0:T(8,128)}, s32[48]{0:T(128)S(1)}, /*index=5*/bf16[12288,256]{...) while((s32[]{:T(128)}, f32[128,256]{1,0:T(8,128)S(1)}, ...), condition=%wide.region_9.10_spmd, body=%wide.region_8.9_spmd.sunk | while | flops 33652744 | bytes 722649 | solution.py:47
  917.5 1.4 convolution_subtract_fusion.11
  966.3 3.6 all_to_all.30
  970.7 3.8 all_to_all.31
  (343 shorter events, 315.6 us)
Async XLA Ops:
  7.2 174.6 %copy-start.2 = (s32[1,48]{1,0:T(1,128)S(1)}, s32[1,48]{1,0:T(1,128)}, u32[]{:S(2)}) copy-start(s32[1,48]{1,0:T(1,128)} %param.13) | copy-start | bytes 580
  7.2 174.5 %all-gather.2.cloned.1.call-start = ((), (), s32[]{:S(2)}) async-start(), calls=%async_computation.2 | async-start | bytes 6299648 | tf_op jit(solution)/shard_map/all_gather | solution.py:59
  7.9 637.4 %all-reduce.2.cloned.1.call-start = ((), (), s32[]{:S(2)}) async-start(), calls=%async_computation.3 | async-start | bytes 524288 | tf_op jit(solution)/shard_map/psum | solution.py:63
  11.3 634.0 %copy-start.1 = (f32[256,256]{1,0:T(8,128)S(1)}, f32[256,256]{1,0:T(8,128)}, u32[]{:S(2)}) copy-start(f32[256,256]{1,0:T(8,128)} %param.12) | copy-start | bytes 786436
  645.3 320.3 %copy-start = (f32[256,256]{1,0:T(8,128)S(1)}, f32[256,256]{1,0:T(8,128)}, u32[]{:S(2)}) copy-start(f32[256,256]{1,0:T(8,128)} %all-reduce.2.cloned.1.call-done) | copy-start | bytes 786436
Sparse Core Ops, SparseCore 0:
  13.6 168.0 all-gather.1
  187.1 458.1 all-reduce.1
where the time goes:
time: 989 us; the launch traced here: 982 us
  waiting for transfers between devices  398 us (40%)
  matrix products  257 us (26%)
  loops' own time  193 us (20%)
  local copies, waits for them, and re-layouts  90.1 us (9%)
  other arithmetic  22.3 us (2%)
  between operations  14.2 us (1%)
    psum x1, waiting for transfers between devices, on_device(): gram_matrix = lax.psum(partial_gram, ('blk', 'grp'))  248 us
    dot_general x144, matrix products, add_slot(): jnp.dot(weighted, item_block, preferred_element_type=jnp.float32)  198 us
    another operation x3, loops' own time, one_block(): lax.fori_loop(0, live_count, add_slot, jnp.zeros(user_rows.shape, jnp.flo...  193 us
    all_gather x1, waiting for transfers between devices, on_device(): gathered = lax.all_gather(item_factors, ('blk', 'grp'), axis=0, tiled=True)  149 us
    dynamic_slice x144, local copies, waits for them, and re-layouts, add_slot(): item_row[turn_index] * tile_width  87.4 us
    dot_general x48, matrix products, add_slot(): jnp.dot(target, item_block, preferred_element_type=jnp.float32)  54.6 us
    mul x1, other arithmetic, confidence_tiles(): return observed * (0.5 + 0.0035 * (hashed // 2 % 1000).astype(jnp.float32))  21.2 us
  transfers between devices with their start and end apart: 2, of which 2 were waited for; matrix products, arithmetic and copies ran while one was open for 18% of the time, Pallas kernels for 0%

commit v1 on v0

v1 whole, which is shorter than its diff:
```python
import jax
import jax.numpy as jnp
from jax import lax
from jax.experimental import pallas as pl
from jax.experimental.pallas import tpu as pltpu
from jax.sharding import PartitionSpec as P

STEPS = 2
NX, NY, NZ = 4, 8, 12
ROWS = 16
RANK = 256
BLOCK = 256
NIB = 48
HALF = RANK // 2
WIDE = 4 * NZ * ROWS
CHUNKS = NX * NY * NZ * ROWS // WIDE
BLOCKS_A_CHUNK = WIDE // 128
PRIME = 65521
SQUARE = 32749 * 32749 % PRIME
ROW_STEP = (7883 * SQUARE + 31) % PRIME
COL_STEP = (6151 * SQUARE + 17) % PRIME
RIDGE = 0.5
MESH = pl.DeviceIdType.MESH


def wrap(value, size):
    return lax.rem(value + size, jnp.int32(size))


def below(value):
    return jnp.where(value >= PRIME, value - PRIME, value)


def kernel(
    items, users, tile_items, tile_seed, tile_count, sol_out, res_out,
    gathered, conf, lane_hash, lane_live, row_hash, gram, total, partial, arrived, vec, solv, resv,
    zs, zr, ys, yr, xs, xr, us, ur, vs, vr, ws, wr, es, er,
):
    blk = lax.axis_index("blk")
    core = lax.axis_index("grp")
    z = lax.rem(blk, NZ)
    line = lax.div(blk, NZ)
    y = lax.rem(line, NY)
    x = lax.div(line, NY)

    def dev(xx, yy, zz, cc=core):
        return ((xx * NY + yy) * NZ + zz, cc)

    def rc(src, dst, send, recv, to):
        return pltpu.make_async_remote_copy(
            src_ref=src, dst_ref=dst, send_sem=send, recv_sem=recv, device_id=to, device_id_type=MESH
        )

    sibling = dev(x, y, z, 1 - core)
    barrier = pltpu.get_barrier_semaphore()

    def greet(to):
        pl.semaphore_signal(barrier, inc=1, device_id=to, device_id_type=MESH)

    def z_line(d, back):
        zz = wrap(z - d, NZ) if back else z
        return rc(items, gathered.at[x, y, zz], zs.at[d - 1], zr.at[d - 1], dev(x, y, wrap(z + d - NZ, NZ)))

    def y_ring(s, sign, back):
        far = s + 1 if back else s
        yy = wrap(y - far, NY) if sign == 0 else wrap(y + far - NY, NY)
        to = dev(x, wrap(y + 1 - NY, NY) if sign == 0 else wrap(y - 1, NY), z)
        ref = gathered.at[x, yy] if s < 3 else gathered.at[x, yy, pl.ds(6 * sign, 6)]
        return rc(ref, ref, ys.at[sign * 4 + s], yr.at[sign * 4 + s], to)

    def x_ring(e, yy, kind, back):
        sign = kind % 2
        far = kind // 2 + (1 if back else 0)
        xx = wrap(x - far, NX) if sign == 0 else wrap(x + far - NX, NX)
        to = dev(wrap(x + 1 - NX, NX) if sign == 0 else wrap(x - 1, NX), y, z)
        ref = gathered.at[xx, yy] if kind < 2 else gathered.at[xx, yy, pl.ds(6 * sign, 6)]
        return rc(ref, ref, xs.at[e * 4 + kind], xr.at[e * 4 + kind], to)

    offsets = (0, -1, 1, -2, 2, -3, 3, 4)

    def y_of(e):
        return wrap(y + offsets[e] - (NY if offsets[e] > 0 else 0), NY)

    def x_send(e):
        for kind in (0, 1):
            x_ring(e, y_of(e), kind, False).start()

    def x_forward(e):
        for kind in (0, 1):
            x_ring(e, y_of(e), kind, True).wait_recv()
            x_ring(e, y_of(e), kind + 2, False).start()

    def x_line(d, back):
        xx = wrap(x - d, NX) if back else x
        return rc(items, gathered.at[xx, y, z], us.at[d - 1], ur.at[d - 1], dev(wrap(x + d - NX, NX), y, z))

    def y_line(d, back):
        yy = wrap(y - d, NY) if back else y
        ref = gathered.at[:, yy, z]
        return rc(ref, ref, vs.at[d - 1], vr.at[d - 1], dev(x, wrap(y + d - NY, NY), z))

    def z_ring(s, k, sign, back):
        far = s + 1 if back else s
        zz = wrap(z - far, NZ) if sign == 0 else wrap(z + far - NZ, NZ)
        to = dev(x, y, wrap(z + 1 - NZ, NZ) if sign == 0 else wrap(z - 1, NZ))
        ref = gathered.at[pl.ds(2 * k, 2), :, zz]
        sem = (s * 2 + k) * 2 + sign
        return rc(ref, ref, ws.at[sem], wr.at[sem], to)

    ring_parts = [[(k, sign) for k in range(2) for sign in range(2)] for _ in range(5)] + [[(0, 0), (1, 1)]]

    gathered[x, y, z] = items[...]

    @pl.when(core == 0)
    def _():
        for d in range(1, NZ):
            greet(dev(x, y, wrap(z + d - NZ, NZ)))
        greet(dev(x, wrap(y + 1 - NY, NY), z))
        greet(dev(x, wrap(y - 1, NY), z))
        greet(dev(wrap(x + 1 - NX, NX), y, z))
        greet(dev(wrap(x - 1, NX), y, z))
        greet(sibling)
        pl.semaphore_wait(barrier, NZ - 1 + 5)
        for d in range(1, NZ):
            z_line(d, False).start()

    @pl.when(core == 1)
    def _():
        for d in range(1, NX):
            greet(dev(wrap(x + d - NX, NX), y, z))
        for d in range(1, NY):
            greet(dev(x, wrap(y + d - NY, NY), z))
        greet(dev(x, y, wrap(z + 1 - NZ, NZ)))
        greet(dev(x, y, wrap(z - 1, NZ)))
        greet(sibling)
        pl.semaphore_wait(barrier, NX - 1 + NY - 1 + 3)
        for d in range(1, NX):
            x_line(d, False).start()

    slot = lax.broadcasted_iota(jnp.int32, (NIB, NIB), 1)
    wanted = lax.broadcasted_iota(jnp.int32, (NIB, NIB), 0)
    seed = lax.rem(lax.rem(lax.rem(tile_seed[...] * 509, PRIME) * 32749, PRIME) * 32749, PRIME)
    match = jnp.where((tile_items[...] == wanted) & (slot < tile_count[0]), 1.0, 0.0)
    live = jnp.sum(match, axis=1, keepdims=True)
    seed_of = jnp.sum(match * seed.astype(jnp.float32), axis=1, keepdims=True).astype(jnp.int32)
    lane = lax.broadcasted_iota(jnp.int32, (NIB, 128), 1)
    column = lax.div(lane, ROWS) * (2 * ROWS) + core * ROWS + lax.rem(lane, ROWS)
    lane_hash[...] = below(lax.rem(column * COL_STEP, PRIME) + seed_of)
    lane_live[...] = jnp.broadcast_to(live, (NIB, 128))
    row_hash[...] = lax.rem(lax.broadcasted_iota(jnp.int32, (BLOCK, 128), 0) * ROW_STEP, PRIME)

    def fill(chunk):
        for piece in range(BLOCKS_A_CHUNK):
            i = chunk * BLOCKS_A_CHUNK + piece
            hashed = below(row_hash[...] + lane_hash[pl.ds(i, 1), :])
            alive = lane_live[pl.ds(i, 1), :]
            value = lax.shift_right_logical(hashed, 1).astype(jnp.float32)
            value = value - 1000.0 * jnp.floor(value * 0.001 + 0.0005)
            weight = 0.5 * alive + (0.0035 * alive) * value
            conf[chunk, :, piece * 128:(piece + 1) * 128] = jnp.where((hashed & 1) == 1, weight, 0.0)

    pl.loop(0, CHUNKS)(fill)

    @pl.when(core == 0)
    def _():
        for d in range(1, NZ):
            z_line(d, True).wait_recv()
        y_ring(0, 0, False).start()
        y_ring(0, 1, False).start()
        x_send(0)
        for s in range(3):
            for sign in (0, 1):
                y_ring(s, sign, True).wait_recv()
                y_ring(s + 1, sign, False).start()
                x_send(2 * s + 1 + sign)
            for e in ((0,), (1, 2), (3, 4))[s]:
                x_forward(e)
        y_ring(3, 0, True).wait_recv()
        y_ring(3, 1, True).wait_recv()
        x_send(7)
        for e in (5, 6, 7):
            x_forward(e)
        for e in range(NY):
            for kind in (2, 3):
                x_ring(e, y_of(e), kind, True).wait_recv()
        for d in range(1, NZ):
            z_line(d, False).wait_send()
        for s in range(4):
            for sign in (0, 1):
                y_ring(s, sign, False).wait_send()
        for e in range(NY):
            for kind in range(4):
                x_ring(e, y_of(e), kind, False).wait_send()

    @pl.when(core == 1)
    def _():
        for d in range(1, NX):
            x_line(d, True).wait_recv()
        for d in range(1, NY):
            y_line(d, False).start()
        for d in range(1, NY):
            y_line(d, True).wait_recv()
        for s in range(6):
            for k, sign in ring_parts[s]:
                if s:
                    z_ring(s - 1, k, sign, True).wait_recv()
                z_ring(s, k, sign, False).start()
        for k, sign in ((0, 1), (1, 0)):
            z_ring(4, k, sign, True).wait_recv()
        for k, sign in ring_parts[5]:
            z_ring(5, k, sign, True).wait_recv()
        for d in range(1, NX):
            x_line(d, False).wait_send()
        for d in range(1, NY):
            y_line(d, False).wait_send()
        for s in range(6):
            for k, sign in ring_parts[s]:
                z_ring(s, k, sign, False).wait_send()

    def item_chunk(chunk):
        rows = gathered[lax.div(chunk, 2), pl.ds(lax.rem(chunk, 2) * 4, 4)]
        return rows.reshape(WIDE, RANK)

    def sweep(first):
        user_rows = vec[...].astype(jnp.bfloat16)

        def add(chunk):
            rows = item_chunk(chunk)
            scores = lax.dot_general(user_rows, rows, (((1,), (1,)), ((), ())), preferred_element_type=jnp.float32)
            trust = conf[chunk]
            weighted = (trust * scores).astype(jnp.bfloat16)
            term = jnp.dot(weighted, rows, preferred_element_type=jnp.float32)
            if first:
                target = jnp.where(trust > 0.0, trust + 1.0, 0.0).astype(jnp.bfloat16)
                total[...] += jnp.dot(target, rows, preferred_element_type=jnp.float32) - term
                gram[...] += lax.dot_general(
                    rows, rows, (((0,), (0,)), ((), ())), preferred_element_type=jnp.float32
                )
            else:
                total[...] += term

        total[...] = jnp.zeros_like(total)
        if first:
            gram[...] = jnp.zeros_like(gram)
        pl.loop(0, CHUNKS)(add)

    def whole(value):
        return jnp.dot(value, gram[...], precision=lax.Precision.HIGHEST, preferred_element_type=jnp.float32)

    def exchange(number, mine):
        partial[number] = mine
        copy = rc(partial.at[number], arrived.at[number], es.at[number], er.at[number], sibling)
        copy.start()
        copy.wait()
        return partial[number] + arrived[number]

    vec[...] = users[...]
    sweep(True)
    start = users[...]
    residual = exchange(0, total[...] - whole(start)) - RIDGE * start
    solv[...] = start
    resv[...] = residual
    vec[...] = residual
    norm = jnp.sum(residual * residual, axis=1, keepdims=True)
    for number in range(STEPS):
        sweep(False)
        applied = exchange(number + 1, whole(vec[...]) + total[...]) + RIDGE * vec[...]
        direction = vec[...]
        step = norm / jnp.sum(direction * applied, axis=1, keepdims=True)
        solv[...] = solv[...] + step * direction
        residual = resv[...] - step * applied
        resv[...] = residual
        following = jnp.sum(residual * residual, axis=1, keepdims=True)
        if number + 1 < STEPS:
            vec[...] = residual + (following / norm) * direction
        norm = following

    for side in (0, 1):
        @pl.when(core == side)
        def _():
            sol_out[...] = solv[:, side * HALF:(side + 1) * HALF]
            res_out[...] = resv[:, side * HALF:(side + 1) * HALF]


def on_device(item_factors, user_start, tile_items, tile_count, tile_seed):
    vmem = pl.BlockSpec(memory_space=pltpu.VMEM)
    whole = (BLOCK, RANK)
    dma = pltpu.SemaphoreType.DMA
    return pl.pallas_call(
        kernel,
        out_shape=[jax.ShapeDtypeStruct((BLOCK, HALF), jnp.float32)] * 2,
        in_specs=[vmem, vmem, vmem, vmem, pl.BlockSpec(memory_space=pltpu.SMEM)],
        out_specs=[vmem, vmem],
        scratch_shapes=[
            pltpu.VMEM((NX, NY, NZ, ROWS, RANK), jnp.bfloat16),
            pltpu.VMEM((CHUNKS, BLOCK, WIDE), jnp.float32),
            pltpu.VMEM((NIB, 128), jnp.int32),
            pltpu.VMEM((NIB, 128), jnp.float32),
            pltpu.VMEM((BLOCK, 128), jnp.int32),
            pltpu.VMEM((RANK, RANK), jnp.float32),
            pltpu.VMEM(whole, jnp.float32),
            pltpu.VMEM((STEPS + 1,) + whole, jnp.float32),
            pltpu.VMEM((STEPS + 1,) + whole, jnp.float32),
            pltpu.VMEM(whole, jnp.float32),
            pltpu.VMEM(whole, jnp.float32),
            pltpu.VMEM(whole, jnp.float32),
            dma((NZ - 1,)), dma((NZ - 1,)),
            dma((8,)), dma((8,)),
            dma((32,)), dma((32,)),
            dma((NX - 1,)), dma((NX - 1,)),
            dma((NY - 1,)), dma((NY - 1,)),
            dma((24,)), dma((24,)),
            dma((STEPS + 1,)), dma((STEPS + 1,)),
        ],
        compiler_params=pltpu.CompilerParams(
            collective_id=0, has_side_effects=True, vmem_limit_bytes=40 * 1024 * 1024
        ),
    )(item_factors, user_start, tile_items, tile_seed, tile_count)


def solution(mesh):
    return jax.shard_map(
        on_device,
        mesh=mesh,
        in_specs=(
            P(("blk", "grp"), None),
            P("blk", None),
            P("blk", None),
            P("blk"),
            P("blk", None),
        ),
        out_specs=(P("blk", "grp"), P("blk", "grp")),
        check_vma=False,
    )
```

time: 989 us -> 74.5 us (0.08)
  the two profiles are of different devices: /device:TPU:669 before, /device:TPU:1 now
where the time goes in v1:
time: 74.5 us; the launch traced here: 74.3 us
  Pallas kernels  70 us (94%)
  local copies, waits for them, and re-layouts  2.96 us (4%)
  between operations  1.34 us (2%)
    pallas_call x1, Pallas kernels, on_device(): pl.pallas_call(kernel, out_shape=[jax.ShapeDtypeStruct((BLOCK, HALF), jnp...  70 us
    unnamed x10, local copies, waits for them, and re-layouts  2.96 us

profile of v1, /device:TPU:1, one launch (start us, length us, event | category | flops | bytes accessed | tf_op | source)
XLA Modules:
  0.0 74.3 jit_solution(1584359335912777562)
XLA Ops:
  0.6 0.0 copy-start.3
  0.6 0.0 copy-start.2
  1.3 0.0 copy-done.3
  1.3 0.0 copy-done.2
  1.3 0.0 copy-start
  1.3 0.9 %copy-done = f32[256,256]{1,0:T(8,128)S(1)} copy-done((f32[256,256]{1,0:T(8,128)S(1)}, f32[256,256]{1,0:T(8,128)}, u32[]{:S(2)}) %copy-start) | copy-done | bytes 262168
  2.3 0.0 copy-start.1
  2.3 0.7 copy-done.1
  3.0 70.0 %shard_map.68 = (f32[256,128]{1,0:T(8,128)S(1)}, f32[256,128]{1,0:T(8,128)S(1)}) custom-call(bf16[16,256]{1,0:T(8,128)(2,1)S(1)} %copy-done.1, f32[256,256]{1,0:T(8,128)S(1)} %copy-done, s32[1,48]{1,0:T(1,128)S(1)} %copy-done.2, s32[1,48]{1,0:T(1,128)S(1)} %copy-done.3, s32[1]{0:T(128)S(6)} %copy.9.tile_count), custom_call_target="tpu_custom_call" | custom-call | tf_op jit(solution)/shard_map/pallas_call | solution.py:289
  73.0 0.7 copy.10
  73.6 0.7 copy.11
Async XLA Ops:
  0.6 0.7 copy-start.3
  0.6 0.7 copy-start.2
  1.3 1.0 %copy-start = (f32[256,256]{1,0:T(8,128)S(1)}, f32[256,256]{1,0:T(8,128)}, u32[]{:S(2)}) copy-start(f32[256,256]{1,0:T(8,128)} %users.1) | copy-start | bytes 786436
  2.3 0.7 copy-start.1

commit v2 on v1

v2 whole, which is shorter than its diff:
```python
import jax
import jax.numpy as jnp
from jax import lax
from jax.experimental import pallas as pl
from jax.experimental.pallas import tpu as pltpu
from jax.sharding import PartitionSpec as P

STEPS = 2
NX, NY, NZ = 4, 8, 12
CHIPS = NX * NY * NZ
ROWS = 16
RANK = 256
BLOCK = 256
NIB = 48
HALF = RANK // 2
GROUPS = CHIPS * ROWS // 128
UNIT = 256
CHUNKS = 8
CHIPS_A_CHUNK = CHIPS // CHUNKS
GROUPS_A_CHUNK = GROUPS // CHUNKS
PRIME = 65521
SQUARE = 32749 * 32749 % PRIME
ROW_STEP = (7883 * SQUARE + 31) % PRIME
COL_STEP = (6151 * SQUARE + 17) % PRIME
RIDGE = 0.5
MESH = pl.DeviceIdType.MESH


def below(value):
    return jnp.where(value >= PRIME, value - PRIME, value)


def matmul(a, b, dims=((1,), (0,))):
    return lax.dot_general(a, b, (dims, ((), ())), preferred_element_type=jnp.float32)


def kernel(
    items, users, tile_items, tile_seed, tile_count, sol_out, res_out,
    gathered, conf, slots, row_hash, gram, total, partial, arrived, vec, vec16, solv, resv,
    s1, r1, s2, r2, s3, r3, es, er, local,
):
    blk = lax.axis_index("blk")
    core = lax.axis_index("grp")
    z = lax.rem(blk, NZ)
    line = lax.div(blk, NZ)
    y = lax.rem(line, NY)
    x = lax.div(line, NY)

    def dev(xx, yy, zz, cc=core):
        return ((xx * NY + yy) * NZ + zz, cc)

    def rc(src, dst, send, recv, to):
        return pltpu.make_async_remote_copy(
            src_ref=src, dst_ref=dst, send_sem=send, recv_sem=recv, device_id=to, device_id_type=MESH
        )

    def around(value, size):
        ahead = [value] + [jnp.where(value + d >= size, value + d - size, value + d) for d in range(1, size)]
        return lambda d: ahead[d % size]

    x_at, y_at, z_at = around(x, NX), around(y, NY), around(z, NZ)

    def by(xd, yd, zd):
        return dev(x_at(xd), y_at(yd), z_at(zd))

    sibling = dev(x, y, z, 1 - core)
    barrier = pltpu.get_barrier_semaphore()

    def greet(to):
        pl.semaphore_signal(barrier, inc=1, device_id=to, device_id_type=MESH)

    def chip0(xx, yy, zz):
        return (yy * NX + xx) * NZ + zz

    def z_line(d, back):
        ref = gathered.at[chip0(x, y, z_at(-d) if back else z)]
        return rc(items, ref, s1.at[d - 1], r1.at[d - 1], by(0, 0, d))

    x_far = (0, 1, -1, 2)

    def x_line(e, back):
        ref = gathered.at[pl.ds(chip0(x_at(-x_far[e]) if back else x, y, 0), NZ)]
        return rc(ref, ref, s2.at[e], r2.at[e], by(x_far[e], 0, 0))

    def y_ring(s, e, side, back):
        sign = 1 - 2 * side
        ref = gathered.at[pl.ds(chip0(x_at(-x_far[e]), y_at(-sign * (s + (1 if back else 0))), 0), NZ)]
        sem = (s * 4 + e) * 2 + side
        return rc(ref, ref, s3.at[sem], r3.at[sem], by(0, sign, 0))

    def chip1(xx, yy, zz):
        return (zz * NX + xx) * NY + yy

    plane = [(xd, yd) for xd in range(NX) for yd in range(NY)][1:]
    plane = sorted(plane, key=lambda m: -min(m[0], NX - m[0]) - min(m[1], NY - m[1]))

    def plane_send(i, back):
        xd, yd = plane[i]
        ref = gathered.at[chip1(x_at(-xd), y_at(-yd), z) if back else chip1(x, y, z)]
        return rc(items, ref, s1.at[i], r1.at[i], by(xd, yd, 0))

    def z_ring(s, e, side, back):
        sign = 1 - 2 * side
        ref = gathered.at[pl.ds(chip1(e, 0, z_at(-sign * (s + (1 if back else 0)))), NY)]
        sem = (s * 4 + e) * 2 + side
        return rc(ref, ref, s3.at[sem], r3.at[sem], by(0, 0, sign))

    def moves(last):
        return [[(e, side) for e in range(NX) for side in (0, 1) if s < last or e % 2 == side] for s in range(last + 1)]

    y_moves, z_moves = moves(NY // 2 - 1), moves(NZ // 2 - 1)

    def fetch(number, src, dst):
        return pltpu.make_async_copy(src, dst, local.at[number])

    own = jnp.where(core == 0, chip0(x, y, z), chip1(x, y, z))
    fetched = [
        fetch(0, items, gathered.at[own]), fetch(1, users, vec),
        fetch(2, tile_items, slots.at[pl.ds(0, 1)]), fetch(3, tile_seed, slots.at[pl.ds(8, 1)]),
    ]
    for copy in fetched:
        copy.start()

    @pl.when(core == 0)
    def _():
        for far in [(0, 0, d) for d in range(1, NZ)] + [(d, 0, 0) for d in range(1, NX)] + [(0, 1, 0), (0, -1, 0)]:
            greet(by(*far))
        greet(sibling)
        pl.semaphore_wait(barrier, NZ - 1 + NX - 1 + 3)
        for d in (6, 5, 7, 4, 8, 3, 9, 2, 10, 1, 11):
            z_line(d, False).start()

    @pl.when(core == 1)
    def _():
        for far in [(xd, yd, 0) for xd, yd in plane] + [(0, 0, 1), (0, 0, -1)]:
            greet(by(*far))
        greet(sibling)
        pl.semaphore_wait(barrier, len(plane) + 3)
        for i in range(len(plane)):
            plane_send(i, False).start()

    for copy in fetched:
        copy.wait()
    start = vec[...]
    vec16[...] = start.astype(jnp.bfloat16)
    total[...] = jnp.zeros_like(total)
    gram[...] = jnp.zeros_like(gram)

    slot = lax.broadcasted_iota(jnp.int32, (NIB, NIB), 1)
    wanted = lax.broadcasted_iota(jnp.int32, (NIB, NIB), 0)
    seeds = slots[8:9, 0:NIB]
    seeds = lax.rem(lax.rem(lax.rem(seeds * 509, PRIME) * 32749, PRIME) * 32749, PRIME)

    def upright(row):
        return jnp.sum(jnp.where(slot == wanted, row.astype(jnp.float32), 0.0), axis=1, keepdims=True)

    seed_col = jnp.broadcast_to(upright(seeds), (NIB, 128))
    item_col = upright(slots[0:1, 0:NIB])
    live_slot = lax.broadcasted_iota(jnp.int32, (NIB, 1), 0) < tile_count[0]
    item_col = jnp.broadcast_to(jnp.where(live_slot, item_col, -1.0), (NIB, 128))
    lane = lax.broadcasted_iota(jnp.int32, (1, 128), 1)
    row_hash[...] = lax.rem(lax.broadcasted_iota(jnp.int32, (BLOCK, 128), 0) * ROW_STEP, PRIME)

    def lanes(group):
        place = group * 8 + lax.div(lane, ROWS)
        yy0, rest0 = lax.div(place, NX * NZ), lax.rem(place, NX * NZ)
        zz1, rest1 = lax.div(place, NX * NY), lax.rem(place, NX * NY)
        chip = jnp.where(
            core == 0,
            (lax.div(rest0, NZ) * NY + yy0) * NZ + lax.rem(rest0, NZ),
            rest1 * NZ + zz1,
        )
        match = jnp.where(item_col == lax.div(chip, 8).astype(jnp.float32), 1.0, 0.0)
        live = jnp.sum(match, axis=0, keepdims=True)
        seed = jnp.sum(match * seed_col, axis=0, keepdims=True).astype(jnp.int32)
        column = lax.rem(chip, 8) * (2 * ROWS) + core * ROWS + lax.rem(lane, ROWS)
        return below(lax.rem(column * COL_STEP, PRIME) + seed), live

    def fill(group):
        offset, alive = lanes(group)
        hashed = below(row_hash[...] + offset)
        value = lax.shift_right_logical(hashed, 1).astype(jnp.float32)
        value = value - 1000.0 * jnp.floor(value * 0.001 + 0.0005)
        weight = 0.5 * alive + (0.0035 * alive) * value
        conf[group] = jnp.where((hashed & 1) == 1, weight, 0.0)

    pl.loop(0, GROUPS)(fill)

    def unit(place):
        rows = gathered[pl.ds(place * (UNIT // ROWS), UNIT // ROWS)].reshape(UNIT, RANK)
        trust = jnp.concatenate([conf[place * 2 + half] for half in range(2)], axis=1)
        scores = matmul(vec16[...], rows, ((1,), (1,)))
        target = jnp.where(trust > 0.0, trust + 1.0, 0.0).astype(jnp.bfloat16)
        wanted_sum = matmul(target, rows)
        gram[...] += matmul(rows, rows, ((0,), (0,)))
        weighted = (trust * scores).astype(jnp.bfloat16)
        total[...] += wanted_sum - matmul(weighted, rows)

    def gather_ring(ring, steps, ready, units_of):
        pending = [(0, part) for part in range(units_of)]

        def some(count):
            for _ in range(min(count, len(pending))):
                far, part = pending.pop(0)
                unit(ready(far) * units_of + part)

        for s in range(len(steps)):
            for e, side in steps[s]:
                if s:
                    ring(s - 1, e, side, True).wait_recv()
                    ring(s, e, side, False).start()
                    if (e, side) != steps[s][0]:
                        some(1)
            if s and s < len(steps) - 1:
                pending.extend((far, part) for far in (-s, s) for part in range(units_of))
        last = len(steps) - 1
        for e, side in steps[last - 1]:
            if (e, side) not in steps[last]:
                ring(last - 1, e, side, True).wait_recv()
        pending.extend((far, part) for far in (-last, last) for part in range(units_of))
        some(2 * units_of)
        for e, side in steps[last]:
            ring(last, e, side, True).wait_recv()
        pending.extend((last + 1, part) for part in range(units_of))
        some(len(pending))

    @pl.when(core == 0)
    def _():
        for d in range(1, NZ):
            z_line(d, True).wait_recv()
        for e in range(1, NX):
            x_line(e, False).start()
        for e in range(NX):
            if e:
                x_line(e, True).wait_recv()
            y_ring(0, e, 0, False).start()
            y_ring(0, e, 1, False).start()
        gather_ring(y_ring, y_moves, y_at, 3)
        for d in range(1, NZ):
            z_line(d, False).wait_send()
        for e in range(1, NX):
            x_line(e, False).wait_send()
        for s in range(len(y_moves)):
            for e, side in y_moves[s]:
                y_ring(s, e, side, False).wait_send()

    @pl.when(core == 1)
    def _():
        for i in range(len(plane)):
            plane_send(i, True).wait_recv()
        for e, side in z_moves[0]:
            z_ring(0, e, side, False).start()
        gather_ring(z_ring, z_moves, z_at, 2)
        for i in range(len(plane)):
            plane_send(i, False).wait_send()
        for s in range(len(z_moves)):
            for e, side in z_moves[s]:
                z_ring(s, e, side, False).wait_send()

    def item_chunk(chunk):
        rows = gathered[pl.ds(chunk * CHIPS_A_CHUNK, CHIPS_A_CHUNK)]
        return rows.reshape(CHIPS_A_CHUNK * ROWS, RANK)

    def sweep():
        user_rows = vec16[...]
        acc = jnp.zeros((BLOCK, RANK), jnp.float32)
        scores = matmul(user_rows, item_chunk(0), ((1,), (1,)))
        for chunk in range(CHUNKS):
            later = matmul(user_rows, item_chunk(chunk + 1), ((1,), (1,))) if chunk + 1 < CHUNKS else None
            trust = jnp.concatenate([conf[chunk * GROUPS_A_CHUNK + k] for k in range(GROUPS_A_CHUNK)], axis=1)
            weighted = (trust * scores).astype(jnp.bfloat16)
            acc = acc + matmul(weighted, item_chunk(chunk))
            scores = later
        return acc

    def whole(value):
        return jnp.dot(value, gram[...], precision=lax.Precision.HIGHEST, preferred_element_type=jnp.float32)

    def exchange(number, mine):
        partial[number] = mine
        copy = rc(partial.at[number], arrived.at[number], es.at[number], er.at[number], sibling)
        copy.start()
        copy.wait()
        return partial[number] + arrived[number]

    start = vec[...]
    residual = exchange(0, total[...] - whole(start)) - RIDGE * start
    solv[...] = start
    resv[...] = residual
    vec[...] = residual
    vec16[...] = residual.astype(jnp.bfloat16)
    norm = jnp.sum(residual * residual, axis=1, keepdims=True)
    for number in range(STEPS):
        applied = exchange(number + 1, sweep() + whole(vec[...])) + RIDGE * vec[...]
        direction = vec[...]
        step = norm / jnp.sum(direction * applied, axis=1, keepdims=True)
        solv[...] = solv[...] + step * direction
        residual = resv[...] - step * applied
        resv[...] = residual
        following = jnp.sum(residual * residual, axis=1, keepdims=True)
        if number + 1 < STEPS:
            direction = residual + (following / norm) * direction
            vec[...] = direction
            vec16[...] = direction.astype(jnp.bfloat16)
        norm = following

    for side in (0, 1):
        @pl.when(core == side)
        def _():
            sol_out[...] = solv[:, side * HALF:(side + 1) * HALF]
            res_out[...] = resv[:, side * HALF:(side + 1) * HALF]


def on_device(item_factors, user_start, tile_items, tile_count, tile_seed):
    vmem = pl.BlockSpec(memory_space=pltpu.VMEM)
    hbm = pl.BlockSpec(memory_space=pltpu.HBM)
    whole = (BLOCK, RANK)
    dma = pltpu.SemaphoreType.DMA
    return pl.pallas_call(
        kernel,
        out_shape=[jax.ShapeDtypeStruct((BLOCK, HALF), jnp.float32)] * 2,
        in_specs=[hbm, hbm, hbm, hbm, pl.BlockSpec(memory_space=pltpu.SMEM)],
        out_specs=[vmem, vmem],
        scratch_shapes=[
            pltpu.VMEM((CHIPS, ROWS, RANK), jnp.bfloat16),
            pltpu.VMEM((GROUPS, BLOCK, 128), jnp.float32),
            pltpu.VMEM((16, NIB), jnp.int32),
            pltpu.VMEM((BLOCK, 128), jnp.int32),
            pltpu.VMEM((RANK, RANK), jnp.float32),
            pltpu.VMEM(whole, jnp.float32),
            pltpu.VMEM((STEPS + 1,) + whole, jnp.float32),
            pltpu.VMEM((STEPS + 1,) + whole, jnp.float32),
            pltpu.VMEM(whole, jnp.float32),
            pltpu.VMEM(whole, jnp.bfloat16),
            pltpu.VMEM(whole, jnp.float32),
            pltpu.VMEM(whole, jnp.float32),
            dma((31,)), dma((31,)),
            dma((NX,)), dma((NX,)),
            dma((48,)), dma((48,)),
            dma((STEPS + 1,)), dma((STEPS + 1,)),
            dma((4,)),
        ],
        compiler_params=pltpu.CompilerParams(
            collective_id=0, has_side_effects=True, vmem_limit_bytes=40 * 1024 * 1024
        ),
    )(item_factors, user_start, tile_items, tile_seed, tile_count)


def solution(mesh):
    return jax.shard_map(
        on_device,
        mesh=mesh,
        in_specs=(
            P(("blk", "grp"), None),
            P("blk", None),
            P("blk", None),
            P("blk"),
            P("blk", None),
        ),
        out_specs=(P("blk", "grp"), P("blk", "grp")),
        check_vma=False,
    )
```

time: 74.5 us -> 64.6 us (0.87)
  Pallas kernels: 70 us -> 60.1 us
    pallas_call x1, Pallas kernels: 70 us -> 60.1 us  [on_device(): pl.pallas_call(kernel, out_shape=[jax.ShapeDtypeStruct((BLOCK, HALF), jnp...]
where the time goes in v2:
time: 64.6 us; the launch traced here: 64.4 us
  Pallas kernels  60.1 us (93%)
  local copies, waits for them, and re-layouts  2.96 us (5%)
  between operations  1.35 us (2%)
    pallas_call x1, Pallas kernels, on_device(): pl.pallas_call(kernel, out_shape=[jax.ShapeDtypeStruct((BLOCK, HALF), jnp...  60.1 us
    unnamed x10, local copies, waits for them, and re-layouts  2.96 us

profile of v2, /device:TPU:1, one launch (start us, length us, event | category | flops | bytes accessed | tf_op | source)
XLA Modules:
  0.0 64.4 jit_solution(1242544510267792692)
XLA Ops:
  0.6 0.0 copy-start.3
  0.6 0.0 copy-start.2
  1.3 0.0 copy-done.3
  1.3 0.0 copy-done.2
  1.3 0.0 copy-start
  1.3 0.9 %copy-done = f32[256,256]{1,0:T(8,128)S(1)} copy-done((f32[256,256]{1,0:T(8,128)S(1)}, f32[256,256]{1,0:T(8,128)}, u32[]{:S(2)}) %copy-start) | copy-done | bytes 262168
  2.3 0.0 copy-start.1
  2.3 0.7 %copy-done.1 = bf16[16,256]{1,0:T(8,128)(2,1)S(1)} copy-done((bf16[16,256]{1,0:T(8,128)(2,1)S(1)}, bf16[16,256]{1,0:T(8,128)(2,1)}, u32[]{:S(2)}) %copy-start.1) | copy-done | bytes 8216
  3.0 60.1 %shard_map.68 = (f32[256,128]{1,0:T(8,128)S(1)}, f32[256,128]{1,0:T(8,128)S(1)}) custom-call(bf16[16,256]{1,0:T(8,128)(2,1)S(1)} %copy-done.1, f32[256,256]{1,0:T(8,128)S(1)} %copy-done, s32[1,48]{1,0:T(1,128)S(1)} %copy-done.2, s32[1,48]{1,0:T(1,128)S(1)} %copy-done.3, s32[1]{0:T(128)S(6)} %copy.9.tile_count), custom_call_target="tpu_custom_call" | custom-call | tf_op jit(solution)/shard_map/pallas_call | solution.py:319
  63.0 0.7 %copy.10 = f32[256,128]{1,0:T(8,128)} copy(f32[256,128]{1,0:T(8,128)S(1)} %get-tuple-element.4) | data formatting | bytes 262144
  63.7 0.7 %copy.11 = f32[256,128]{1,0:T(8,128)} copy(f32[256,128]{1,0:T(8,128)S(1)} %get-tuple-element.5) | data formatting | bytes 262144
Async XLA Ops:
  0.6 0.7 %copy-start.3 = (s32[1,48]{1,0:T(1,128)S(1)}, s32[1,48]{1,0:T(1,128)}, u32[]{:S(2)}) copy-start(s32[1,48]{1,0:T(1,128)} %tile_seed.1) | copy-start | bytes 580
  0.6 0.7 %copy-start.2 = (s32[1,48]{1,0:T(1,128)S(1)}, s32[1,48]{1,0:T(1,128)}, u32[]{:S(2)}) copy-start(s32[1,48]{1,0:T(1,128)} %tile_items.1) | copy-start | bytes 580
  1.3 1.0 %copy-start = (f32[256,256]{1,0:T(8,128)S(1)}, f32[256,256]{1,0:T(8,128)}, u32[]{:S(2)}) copy-start(f32[256,256]{1,0:T(8,128)} %users.1) | copy-start | bytes 786436
  2.3 0.7 %copy-start.1 = (bf16[16,256]{1,0:T(8,128)(2,1)S(1)}, bf16[16,256]{1,0:T(8,128)(2,1)}, u32[]{:S(2)}) copy-start(bf16[16,256]{1,0:T(8,128)(2,1)} %items.1) | copy-start | bytes 24580

commit v3 on v2

--- a/solution.py
+++ b/solution.py
@@ -36,7 +36,7 @@
 
 def kernel(
     items, users, tile_items, tile_seed, tile_count, sol_out, res_out,
-    gathered, conf, slots, row_hash, gram, total, partial, arrived, vec, vec16, solv, resv,
+    gathered, conf, slots, row_hash, gram, gram_other, gram_sum, total, partial, arrived, vec, vec16, solv, resv,
     s1, r1, s2, r2, s3, r3, es, er, local,
 ):
     blk = lax.axis_index("blk")
@@ -84,8 +84,9 @@
 
     def y_ring(s, e, side, back):
         sign = 1 - 2 * side
-        ref = gathered.at[pl.ds(chip0(x_at(-x_far[e]), y_at(-sign * (s + (1 if back else 0))), 0), NZ)]
-        sem = (s * 4 + e) * 2 + side
+        place = chip0(x_at(-x_far[e // 2]), y_at(-sign * (s + (1 if back else 0))), e % 2 * 6)
+        ref = gathered.at[pl.ds(place, 6)]
+        sem = (s * 8 + e) * 2 + side
         return rc(ref, ref, s3.at[sem], r3.at[sem], by(0, sign, 0))
 
     def chip1(xx, yy, zz):
@@ -105,10 +106,10 @@
         sem = (s * 4 + e) * 2 + side
         return rc(ref, ref, s3.at[sem], r3.at[sem], by(0, 0, sign))
 
-    def moves(last):
-        return [[(e, side) for e in range(NX) for side in (0, 1) if s < last or e % 2 == side] for s in range(last + 1)]
-
-    y_moves, z_moves = moves(NY // 2 - 1), moves(NZ // 2 - 1)
+    def moves(last, subs):
+        return [[(e, side) for e in range(subs) for side in (0, 1) if s < last or e % 2 == side] for s in range(last + 1)]
+
+    y_moves, z_moves = moves(NY // 2 - 1, 2 * NX), moves(NZ // 2 - 1, NX)
 
     def fetch(number, src, dst):
         return pltpu.make_async_copy(src, dst, local.at[number])
@@ -233,8 +234,9 @@
         for e in range(NX):
             if e:
                 x_line(e, True).wait_recv()
-            y_ring(0, e, 0, False).start()
-            y_ring(0, e, 1, False).start()
+            for piece in range(2):
+                y_ring(0, 2 * e + piece, 0, False).start()
+                y_ring(0, 2 * e + piece, 1, False).start()
         gather_ring(y_ring, y_moves, y_at, 3)
         for d in range(1, NZ):
             z_line(d, False).wait_send()
@@ -273,26 +275,35 @@
             scores = later
         return acc
 
-    def whole(value):
-        return jnp.dot(value, gram[...], precision=lax.Precision.HIGHEST, preferred_element_type=jnp.float32)
-
-    def exchange(number, mine):
-        partial[number] = mine
-        copy = rc(partial.at[number], arrived.at[number], es.at[number], er.at[number], sibling)
-        copy.start()
-        copy.wait()
-        return partial[number] + arrived[number]
+    def whole(value, matrix):
+        return jnp.dot(value, matrix, precision=lax.Precision.HIGHEST, preferred_element_type=jnp.float32)
+
+    copies = [
+        rc(partial.at[number], arrived.at[number], es.at[number], er.at[number], sibling) for number in range(STEPS + 1)
+    ]
+    gram_copy = rc(gram, gram_other, es.at[STEPS + 1], er.at[STEPS + 1], sibling)
 
     start = vec[...]
-    residual = exchange(0, total[...] - whole(start)) - RIDGE * start
+    partial[0] = total[...] - whole(start, gram[...])
+    copies[0].start()
+    gram_copy.start()
+    copies[0].wait_recv()
+    residual = partial[0] + arrived[0] - RIDGE * start
     solv[...] = start
     resv[...] = residual
     vec[...] = residual
     vec16[...] = residual.astype(jnp.bfloat16)
     norm = jnp.sum(residual * residual, axis=1, keepdims=True)
     for number in range(STEPS):
-        applied = exchange(number + 1, sweep() + whole(vec[...])) + RIDGE * vec[...]
+        partial[number + 1] = sweep()
+        copies[number + 1].start()
+        if number == 0:
+            gram_copy.wait_recv()
+            gram_sum[...] = gram[...] + gram_other[...]
         direction = vec[...]
+        applied = whole(direction, gram_sum[...]) + RIDGE * direction
+        copies[number + 1].wait_recv()
+        applied = applied + (partial[number + 1] + arrived[number + 1])
         step = norm / jnp.sum(direction * applied, axis=1, keepdims=True)
         solv[...] = solv[...] + step * direction
         residual = resv[...] - step * applied
@@ -303,6 +314,9 @@
             vec[...] = direction
             vec16[...] = direction.astype(jnp.bfloat16)
         norm = following
+
+    for copy in copies + [gram_copy]:
+        copy.wait_send()
 
     for side in (0, 1):
         @pl.when(core == side)
@@ -327,6 +341,8 @@
             pltpu.VMEM((16, NIB), jnp.int32),
             pltpu.VMEM((BLOCK, 128), jnp.int32),
             pltpu.VMEM((RANK, RANK), jnp.float32),
+            pltpu.VMEM((RANK, RANK), jnp.float32),
+            pltpu.VMEM((RANK, RANK), jnp.float32),
             pltpu.VMEM(whole, jnp.float32),
             pltpu.VMEM((STEPS + 1,) + whole, jnp.float32),
             pltpu.VMEM((STEPS + 1,) + whole, jnp.float32),
@@ -336,8 +352,8 @@
             pltpu.VMEM(whole, jnp.float32),
             dma((31,)), dma((31,)),
             dma((NX,)), dma((NX,)),
-            dma((48,)), dma((48,)),
-            dma((STEPS + 1,)), dma((STEPS + 1,)),
+            dma((64,)), dma((64,)),
+            dma((STEPS + 2,)), dma((STEPS + 2,)),
             dma((4,)),
         ],
         compiler_params=pltpu.CompilerParams(

time: 64.6 us -> 64.4 us (level)
  no operation moved by 1% of the time
where the time goes in v3:
time: 64.4 us; the launch traced here: 64.2 us
  Pallas kernels  59.9 us (93%)
  local copies, waits for them, and re-layouts  2.96 us (5%)
  between operations  1.35 us (2%)
    pallas_call x1, Pallas kernels, on_device(): pl.pallas_call(kernel, out_shape=[jax.ShapeDtypeStruct((BLOCK, HALF), jnp...  59.9 us
    unnamed x10, local copies, waits for them, and re-layouts  2.96 us

profile of v3, /device:TPU:1, one launch (start us, length us, event | category | flops | bytes accessed | tf_op | source)
XLA Modules:
  0.0 64.2 jit_solution(12008419464768221073)
XLA Ops:
  0.6 0.0 copy-start.3
  0.6 0.0 copy-start.2
  1.3 0.0 copy-done.3
  1.3 0.0 copy-done.2
  1.3 0.0 copy-start
  1.3 0.9 %copy-done = f32[256,256]{1,0:T(8,128)S(1)} copy-done((f32[256,256]{1,0:T(8,128)S(1)}, f32[256,256]{1,0:T(8,128)}, u32[]{:S(2)}) %copy-start) | copy-done | bytes 262168
  2.3 0.0 copy-start.1
  2.3 0.7 %copy-done.1 = bf16[16,256]{1,0:T(8,128)(2,1)S(1)} copy-done((bf16[16,256]{1,0:T(8,128)(2,1)S(1)}, bf16[16,256]{1,0:T(8,128)(2,1)}, u32[]{:S(2)}) %copy-start.1) | copy-done | bytes 8216
  3.0 59.9 %shard_map.68 = (f32[256,128]{1,0:T(8,128)S(1)}, f32[256,128]{1,0:T(8,128)S(1)}) custom-call(bf16[16,256]{1,0:T(8,128)(2,1)S(1)} %copy-done.1, f32[256,256]{1,0:T(8,128)S(1)} %copy-done, s32[1,48]{1,0:T(1,128)S(1)} %copy-done.2, s32[1,48]{1,0:T(1,128)S(1)} %copy-done.3, s32[1]{0:T(128)S(6)} %copy.9.tile_count), custom_call_target="tpu_custom_call" | custom-call | tf_op jit(solution)/shard_map/pallas_call | solution.py:333
  62.9 0.7 %copy.10 = f32[256,128]{1,0:T(8,128)} copy(f32[256,128]{1,0:T(8,128)S(1)} %get-tuple-element.4) | data formatting | bytes 262144
  63.6 0.7 %copy.11 = f32[256,128]{1,0:T(8,128)} copy(f32[256,128]{1,0:T(8,128)S(1)} %get-tuple-element.5) | data formatting | bytes 262144
Async XLA Ops:
  0.6 0.7 %copy-start.3 = (s32[1,48]{1,0:T(1,128)S(1)}, s32[1,48]{1,0:T(1,128)}, u32[]{:S(2)}) copy-start(s32[1,48]{1,0:T(1,128)} %tile_seed.1) | copy-start | bytes 580
  0.6 0.7 %copy-start.2 = (s32[1,48]{1,0:T(1,128)S(1)}, s32[1,48]{1,0:T(1,128)}, u32[]{:S(2)}) copy-start(s32[1,48]{1,0:T(1,128)} %tile_items.1) | copy-start | bytes 580
  1.3 1.0 %copy-start = (f32[256,256]{1,0:T(8,128)S(1)}, f32[256,256]{1,0:T(8,128)}, u32[]{:S(2)}) copy-start(f32[256,256]{1,0:T(8,128)} %users.1) | copy-start | bytes 786436
  2.3 0.7 %copy-start.1 = (bf16[16,256]{1,0:T(8,128)(2,1)S(1)}, bf16[16,256]{1,0:T(8,128)(2,1)}, u32[]{:S(2)}) copy-start(bf16[16,256]{1,0:T(8,128)(2,1)} %items.1) | copy-start | bytes 24580

commit v4 on v2

--- a/solution.py
+++ b/solution.py
@@ -70,21 +70,19 @@
         pl.semaphore_signal(barrier, inc=1, device_id=to, device_id_type=MESH)
 
     def chip0(xx, yy, zz):
-        return (yy * NX + xx) * NZ + zz
+        return (yy * NZ + zz) * NX + xx
+
+    def x_line(d, back):
+        ref = gathered.at[chip0(x_at(-d) if back else x, y, z)]
+        return rc(items, ref, s1.at[d - 1], r1.at[d - 1], by(d, 0, 0))
 
     def z_line(d, back):
-        ref = gathered.at[chip0(x, y, z_at(-d) if back else z)]
-        return rc(items, ref, s1.at[d - 1], r1.at[d - 1], by(0, 0, d))
-
-    x_far = (0, 1, -1, 2)
-
-    def x_line(e, back):
-        ref = gathered.at[pl.ds(chip0(x_at(-x_far[e]) if back else x, y, 0), NZ)]
-        return rc(ref, ref, s2.at[e], r2.at[e], by(x_far[e], 0, 0))
+        ref = gathered.at[pl.ds(chip0(0, y, z_at(-d) if back else z), NX)]
+        return rc(ref, ref, s2.at[d - 1], r2.at[d - 1], by(0, 0, d))
 
     def y_ring(s, e, side, back):
         sign = 1 - 2 * side
-        ref = gathered.at[pl.ds(chip0(x_at(-x_far[e]), y_at(-sign * (s + (1 if back else 0))), 0), NZ)]
+        ref = gathered.at[pl.ds(chip0(0, y_at(-sign * (s + (1 if back else 0))), 3 * e), 3 * NX)]
         sem = (s * 4 + e) * 2 + side
         return rc(ref, ref, s3.at[sem], r3.at[sem], by(0, sign, 0))
 
@@ -127,8 +125,8 @@
             greet(by(*far))
         greet(sibling)
         pl.semaphore_wait(barrier, NZ - 1 + NX - 1 + 3)
-        for d in (6, 5, 7, 4, 8, 3, 9, 2, 10, 1, 11):
-            z_line(d, False).start()
+        for d in (2, 1, 3):
+            x_line(d, False).start()
 
     @pl.when(core == 1)
     def _():
@@ -167,7 +165,7 @@
         zz1, rest1 = lax.div(place, NX * NY), lax.rem(place, NX * NY)
         chip = jnp.where(
             core == 0,
-            (lax.div(rest0, NZ) * NY + yy0) * NZ + lax.rem(rest0, NZ),
+            (lax.rem(rest0, NX) * NY + yy0) * NZ + lax.div(rest0, NX),
             rest1 * NZ + zz1,
         )
         match = jnp.where(item_col == lax.div(chip, 8).astype(jnp.float32), 1.0, 0.0)
@@ -226,20 +224,19 @@
 
     @pl.when(core == 0)
     def _():
+        for d in range(1, NX):
+            x_line(d, True).wait_recv()
+        for d in (6, 5, 7, 4, 8, 3, 9, 2, 10, 1, 11):
+            z_line(d, False).start()
         for d in range(1, NZ):
             z_line(d, True).wait_recv()
-        for e in range(1, NX):
-            x_line(e, False).start()
-        for e in range(NX):
-            if e:
-                x_line(e, True).wait_recv()
-            y_ring(0, e, 0, False).start()
-            y_ring(0, e, 1, False).start()
+        for e, side in y_moves[0]:
+            y_ring(0, e, side, False).start()
         gather_ring(y_ring, y_moves, y_at, 3)
         for d in range(1, NZ):
             z_line(d, False).wait_send()
-        for e in range(1, NX):
-            x_line(e, False).wait_send()
+        for d in range(1, NX):
+            x_line(d, False).wait_send()
         for s in range(len(y_moves)):
             for e, side in y_moves[s]:
                 y_ring(s, e, side, False).wait_send()
@@ -335,7 +332,7 @@
             pltpu.VMEM(whole, jnp.float32),
             pltpu.VMEM(whole, jnp.float32),
             dma((31,)), dma((31,)),
-            dma((NX,)), dma((NX,)),
+            dma((NZ - 1,)), dma((NZ - 1,)),
             dma((48,)), dma((48,)),
             dma((STEPS + 1,)), dma((STEPS + 1,)),
             dma((4,)),

time: 64.6 us -> 71 us (1.099)
  Pallas kernels: 60.1 us -> 66.5 us
    pallas_call x1, Pallas kernels: 60.1 us -> 66.5 us  [on_device(): pl.pallas_call(kernel, out_shape=[jax.ShapeDtypeStruct((BLOCK, HALF), jnp...]
where the time goes in v4:
time: 71 us; the launch traced here: 70.8 us
  Pallas kernels  66.5 us (94%)
  local copies, waits for them, and re-layouts  2.96 us (4%)
  between operations  1.35 us (2%)
    pallas_call x1, Pallas kernels, on_device(): pl.pallas_call(kernel, out_shape=[jax.ShapeDtypeStruct((BLOCK, HALF), jnp...  66.5 us
    unnamed x10, local copies, waits for them, and re-layouts  2.96 us

profile of v4, /device:TPU:1, one launch (start us, length us, event | category | flops | bytes accessed | tf_op | source)
XLA Modules:
  0.0 70.8 jit_solution(4659387711735345012)
XLA Ops:
  0.6 0.0 copy-start.3
  0.6 0.0 copy-start.2
  1.3 0.0 copy-done.3
  1.3 0.0 copy-done.2
  1.3 0.0 copy-start
  1.3 0.9 %copy-done = f32[256,256]{1,0:T(8,128)S(1)} copy-done((f32[256,256]{1,0:T(8,128)S(1)}, f32[256,256]{1,0:T(8,128)}, u32[]{:S(2)}) %copy-start) | copy-done | bytes 262168
  2.3 0.0 copy-start.1
  2.3 0.7 copy-done.1
  3.0 66.5 %shard_map.68 = (f32[256,128]{1,0:T(8,128)S(1)}, f32[256,128]{1,0:T(8,128)S(1)}) custom-call(bf16[16,256]{1,0:T(8,128)(2,1)S(1)} %copy-done.1, f32[256,256]{1,0:T(8,128)S(1)} %copy-done, s32[1,48]{1,0:T(1,128)S(1)} %copy-done.2, s32[1,48]{1,0:T(1,128)S(1)} %copy-done.3, s32[1]{0:T(128)S(6)} %copy.9.tile_count), custom_call_target="tpu_custom_call" | custom-call | tf_op jit(solution)/shard_map/pallas_call | solution.py:316
  69.5 0.7 copy.10
  70.1 0.7 copy.11
Async XLA Ops:
  0.6 0.7 copy-start.3
  0.6 0.7 copy-start.2
  1.3 1.0 %copy-start = (f32[256,256]{1,0:T(8,128)S(1)}, f32[256,256]{1,0:T(8,128)}, u32[]{:S(2)}) copy-start(f32[256,256]{1,0:T(8,128)} %users.1) | copy-start | bytes 786436
  2.3 0.7 copy-start.1
